TPU v7x, 256 devices: a whole 4x4x8 slice. The times are simulated.
256 devices in a mesh: axial: 8 (over z_lo, x), sector: 32 (over y, z_hi, core).
Axes of the slice: x: 4, y: 4, z: 8 (z_hi: 4, z_lo: 2; z = z_hi * 2 + z_lo), core: 2. Of those that a mesh axis runs over, the one named last changes fastest.
Arguments:
- state: float32 [5, 6, 6, 6, 8, 32, 128], P(None, None, None, None, 'axial', 'sector'), may hold values from -0.6 to 0.6
- register: float32 [5, 6, 6, 6, 8, 32, 128], P(None, None, None, None, 'axial', 'sector'), may hold values from -6 to 6
- flux_x: float32 [5, 5], replicated, may hold values from -2.5 to 2.5
- flux_y: float32 [5, 5], replicated, may hold values from -2.5 to 2.5
- flux_z: float32 [5, 5], replicated, may hold values from -2.5 to 2.5
- viscosity: float32 [5], replicated, may hold values from 0.01 to 0.1
- mortar_partner: int32 [2, 32], P(None, 'sector'), may hold values from 0 to 31, as said below
Outputs:
- state_new: float32 [5, 6, 6, 6, 8, 32, 128], P(None, None, None, None, 'axial', 'sector')
- register_new: float32 [5, 6, 6, 6, 8, 32, 128], P(None, None, None, None, 'axial', 'sector')
Inputs may be any that keep to these rules, and one draw needn't show every extreme that they name: The interface is a rotation by one whole number s of elements plus half an element: mortar_partner[0, c] = (c + s) mod 32 and mortar_partner[1, c] = (c - s - 1) mod 32 for every c, with the same s in both rows.
All inputs are finite; a program needn't handle non-finite values.
Results may differ from a plain program's by a relative error of at most 0.0003.
Values sent between devices are 32-bit elements; how exact they have to be, the bound alone decides.
A program may use at most 64 MiB of HBM per device.

v0:
```python
import functools

import jax
import jax.numpy as jnp
import numpy as np
from jax import lax
from jax.experimental import pallas as pl
from jax.experimental.pallas import tpu as pltpu
from jax.sharding import PartitionSpec as P

NODES = (
    -1.0,
    -0.7650553239294647,
    -0.2852315164806451,
    0.2852315164806451,
    0.7650553239294647,
    1.0,
)
WEIGHTS = (
    1.0 / 15.0,
    0.378474956297847,
    0.5548583770354863,
    0.5548583770354863,
    0.378474956297847,
    1.0 / 15.0,
)
half_gain = 7.5
step_size = 0.01
section_a = -0.4178904745
section_b = 1.5306374668
MESH = pl.DeviceIdType.MESH

NV = 5
NN = 6
FACE = NN * NN
BODY = NN * FACE
BODY_PAD = 224
LANES = 128
WIDE = NV * LANES
ROOM = WIDE + LANES
MSG = 2 * FACE
HEAD = 40
BLOCK = HEAD + MSG
TAIL = 32
MORT_K = 368
Z_FACE = 4 * BLOCK
OWN = 6 * BLOCK
TABLE = OWN + 4 * BODY
CHUNK = 256


def basis_tables():
    points = np.array(NODES)
    weights = np.array(WEIGHTS)
    count = points.shape[0]
    barycentric = np.array(
        [
            1.0
            / np.prod([points[first] - points[other] for other in range(count) if other != first])
            for first in range(count)
        ]
    )
    derivative = np.zeros((count, count))
    for target in range(count):
        for source in range(count):
            if source != target:
                derivative[target, source] = (
                    barycentric[source] / barycentric[target] / (points[target] - points[source])
                )
        derivative[target, target] = -np.sum(derivative[target])

    def lagrange(places):
        result = np.ones((count, count))
        for column in range(count):
            for other in range(count):
                if other != column:
                    result[:, column] *= (places - points[other]) / (points[column] - points[other])
        return result

    lower_map = lagrange((points - 1.0) / 2.0)
    upper_map = lagrange((points + 1.0) / 2.0)
    back_lower = 0.5 * lower_map.T * weights[None, :] / weights[:, None]
    back_upper = 0.5 * upper_map.T * weights[None, :] / weights[:, None]
    return derivative, lower_map, upper_map, back_lower, back_upper


def along(matrix, dimension):
    parts = [np.eye(NN)] * 3
    parts[dimension] = matrix
    return np.kron(np.kron(parts[0], parts[1]), parts[2])


def operators():
    derivative, lower_map, upper_map, back_lower, back_upper = basis_tables()
    eye = np.eye(NN)
    first, last = eye[:1], eye[-1:]

    body = np.zeros((4 * BODY, BODY_PAD))
    second = np.zeros((BODY, BODY))
    for d in range(3):
        own = derivative + half_gain * (first.T @ first - last.T @ last)
        twice = derivative @ own + half_gain * (
            first.T @ derivative[:1] - last.T @ derivative[-1:]
        )
        body[d * BODY : (d + 1) * BODY, :BODY] = along(own, d)
        second += along(twice, d)
    body[3 * BODY :, :BODY] = second

    face = np.zeros((6 * BLOCK, BODY_PAD))
    far = np.zeros((3, BODY_PAD, 2 * MSG))
    for d in range(3):
        for end in range(2):
            row = first if end == 0 else last
            slope = derivative[:1] if end == 0 else derivative[-1:]
            sign = 1.0 if end == 0 else -1.0
            at = (2 * d + end) * BLOCK
            trace = along(row, d)
            face[at : at + FACE, :BODY] = trace
            face[at + HEAD : at + HEAD + FACE, :BODY] = sign * half_gain * along(slope, d)
            face[at + HEAD + FACE : at + BLOCK, :BODY] = half_gain * trace
            to = end * MSG
            column = derivative[:, :1] if end == 0 else derivative[:, -1:]
            far[d, :BODY, to : to + FACE] = trace.T
            far[d, :BODY, to + FACE : to + MSG] = -sign * along(column, d)

    low = back_lower @ upper_map
    high = back_upper @ lower_map
    same = back_lower @ lower_map + back_upper @ upper_map
    less = same - 2.0 * eye

    def on_face(matrix):
        return np.kron(matrix, eye)

    mortar = np.zeros((2, 80, MORT_K))
    b, c = slice(0, FACE), slice(FACE, MSG)
    skip = FACE - TAIL
    for straight_low in range(2):

        def put(rows, at, matrix):
            mortar[straight_low, rows, at : at + FACE] = on_face(matrix)

        low_at, high_at = (MSG, 3 * MSG) if straight_low else (2 * MSG, MSG)
        put(b, 0, eye - same)
        put(b, FACE, half_gain * (less @ less - low @ high - high @ low))
        put(c, FACE, same - eye)
        for matrix, at in ((low, low_at), (high, high_at)):
            put(b, at, matrix)
            put(b, at + FACE, half_gain * (less @ matrix - matrix @ less))
            put(c, at + FACE, matrix)
        put(b, 4 * MSG + skip, -half_gain * (low @ low))
        put(b, 4 * MSG + HEAD + skip, -half_gain * (high @ high))
    return face, body, far, mortar


def thirds(matrix):
    high = np.asarray(matrix, np.float32).astype(jnp.bfloat16)
    low = (matrix - high.astype(np.float64)).astype(np.float32).astype(jnp.bfloat16)
    return np.concatenate([high, high, low], axis=-1)


def put_box(box, lanes, value):
    rows = value.shape[0]
    high = value.astype(jnp.bfloat16)
    box[0:rows, lanes] = high
    box[rows : 2 * rows, lanes] = (value - high.astype(jnp.float32)).astype(jnp.bfloat16)
    box[2 * rows : 3 * rows, lanes] = high


def place_of(counts):
    axial_count = counts[0]
    half = axial_count // 2
    me = lax.axis_index("axial")
    is_rotor = me == half - 1
    is_mortar = jnp.logical_or(me == half - 1, me == half)
    has_left = jnp.logical_and(me != 0, me != half)
    has_right = jnp.logical_and(me != axial_count - 1, me != half - 1)
    return me, is_rotor, is_mortar, has_left, has_right


def columns(v):
    return slice(v * LANES, (v + 1) * LANES)


def exchange(
    shift,
    counts,
    odd,
    state_hbm,
    body_hbm,
    far_hbm,
    mortar_hbm,
    edge_hbm,
    flux_x_hbm,
    flux_y_hbm,
    flux_z_hbm,
    viscosity_hbm,
    residual_hbm,
    state,
    body_op,
    far_op,
    mortar_op,
    edge,
    flux,
    viscosity,
    speed,
    message,
    box,
    inbox,
    mortar_in,
    mortar_box,
    stand_in,
    z_message,
    far_box,
    local,
    total,
    load_sem,
    local_sem,
    send_sem,
    recv_sem,
):
    axial_count, sectors = counts
    half = axial_count // 2
    me, is_rotor, is_mortar, has_left, has_right = place_of(counts)
    is_end = jnp.logical_or(me == 0, me == axial_count - 1)
    place = lax.axis_index("sector")
    after = lax.rem(place + 1, sectors)
    before = lax.rem(place + sectors - 1, sectors)
    turn = 2 * shift + 1
    across = lax.rem(
        place + jnp.where(is_rotor, turn % sectors, (sectors - turn) % sectors), sectors
    )
    other_row = jnp.where(is_rotor, half, half - 1)
    own = jnp.where(is_rotor, 1, 0)

    barrier = pltpu.get_barrier_semaphore()

    def greet(row, column):
        pl.semaphore_signal(barrier, inc=1, device_id=(row, column), device_id_type=MESH)

    @pl.when(is_mortar)
    def _():
        greet(other_row, across)

    greet(me, after)
    greet(me, before)

    @pl.when(has_left)
    def _():
        greet(me - 1, place)

    @pl.when(has_right)
    def _():
        greet(me + 1, place)

    loads = [
        pltpu.make_async_copy(origin, target, load_sem.at[k])
        for k, (origin, target) in enumerate(
            (
                (state_hbm, state),
                (body_hbm.at[0:CHUNK], body_op.at[0:CHUNK]),
                (flux_x_hbm, flux.at[0]),
                (flux_y_hbm, flux.at[1]),
                (viscosity_hbm, viscosity),
                (flux_z_hbm, flux.at[2]),
                (body_hbm.at[CHUNK:], body_op.at[CHUNK:]),
                (far_hbm, far_op),
                (edge_hbm, edge),
                (mortar_hbm, mortar_op),
            )
        )
    ]
    for load in loads:
        load.start()

    def remote(origin, target, k, row, column):
        return pltpu.make_async_remote_copy(
            src_ref=origin,
            dst_ref=target,
            send_sem=send_sem.at[k],
            recv_sem=recv_sem.at[k],
            device_id=(row, column),
            device_id_type=MESH,
        )

    from_left = inbox.at[0:MSG]
    from_right = inbox.at[MSG : 2 * MSG]
    from_before = inbox.at[2 * MSG : 3 * MSG]
    from_after = inbox.at[3 * MSG : 4 * MSG]
    go_right = remote(message.at[1], from_left, 0, me + 1, place)
    go_left = remote(message.at[0], from_right, 1, me - 1, place)
    go_after = remote(message.at[3], from_before, 2, me, after)
    go_before = remote(message.at[2], from_after, 3, me, before)
    tail = message.at[own, TAIL:]
    row_after = remote(tail, mortar_in.at[4 * MSG : 4 * MSG + HEAD], 4, me, after)
    row_before = remote(
        tail, mortar_in.at[4 * MSG + HEAD : 4 * MSG + 2 * HEAD], 5, me, before
    )

    pieces = []
    for k, (start, stop) in enumerate(((0, HEAD), (HEAD, MSG))):

        def box_at(part):
            return mortar_in.at[part * MSG + start : part * MSG + stop]

        pieces.append(
            (
                remote(message.at[own, start:stop], box_at(1), 6 + k, other_row, across),
                remote(box_at(1), box_at(2), 8 + k, me, after),
                remote(box_at(1), box_at(3), 10 + k, me, before),
            )
        )

    keep = pltpu.make_async_copy(message.at[own], mortar_in.at[0:MSG], local_sem.at[0])
    end_slot = pl.multiple_of(jnp.where(me == 0, 0, MSG), 8)
    close = pltpu.make_async_copy(message.at[4], inbox.at[pl.ds(end_slot, MSG)], local_sem.at[1])

    loads[0].wait()

    def pair(k):
        return pl.ds(pl.multiple_of(k * 2 * LANES, 2 * LANES), 2 * LANES)

    def one(v):
        return pl.ds(pl.multiple_of(v * LANES, LANES), LANES)

    pairs = (NV + 1) // 2

    def split_one(v, carry):
        whole = jnp.concatenate(
            [state[v], jnp.zeros((BODY_PAD - BODY, LANES), jnp.float32)], axis=0
        )
        put_box(box, one(v), whole)
        return carry

    lax.fori_loop(0, NV, split_one, 0)
    for load in loads[1:6]:
        load.wait()

    def find_speed(d, carry):
        largest = jnp.float32(0.0)
        for row in range(NV):
            entry = jnp.abs(flux[d, row, 0])
            for column in range(1, NV):
                entry = entry + jnp.abs(flux[d, row, column])
            largest = jnp.maximum(largest, entry)
        speed[d] = half_gain * largest
        return carry

    lax.fori_loop(0, 3, find_speed, 0)

    def make_message(origin, base, d, end, v, target, face):
        gain = jnp.where(end == 1, half_gain, -half_gain)
        at = pl.multiple_of(base, 8)
        lanes = one(v)
        mixed = speed[d] * origin[pl.ds(at, HEAD), lanes]
        for w in range(NV):
            mixed = mixed + (gain * flux[d, v, w]) * origin[pl.ds(at, HEAD), columns(w)]
        part = viscosity[v] * origin[pl.ds(pl.multiple_of(at + HEAD, 8), MSG), lanes]
        target[face, :HEAD, lanes] = part[:HEAD] + mixed
        target[face, HEAD:, lanes] = part[HEAD:]

    def send_face(face, carry):
        def make(v, carry):
            make_message(local, face * BLOCK, face // 2, lax.rem(face, 2), v, message, face)
            return carry

        lax.fori_loop(0, NV, make, 0)

        @pl.when(face == 1)
        def _():
            pl.semaphore_wait(barrier, jnp.where(is_mortar, 4, jnp.where(is_end, 3, 4)))

            @pl.when(is_mortar)
            def _():
                for send, _, _ in pieces:
                    send.start()
                row_after.start()
                row_before.start()
                keep.start()

            @pl.when(has_right)
            def _():
                go_right.start()

            @pl.when(has_left)
            def _():
                go_left.start()

        @pl.when(face == 3)
        def _():
            go_after.start()
            go_before.start()

        return carry

    def close_end():
        at = pl.multiple_of(jnp.where(me == 0, 0, BLOCK), 8)

        def close_one(v, carry):
            message[4, :HEAD, one(v)] = (half_gain * half_gain * viscosity[v]) * local[
                pl.ds(at, HEAD), one(v)
            ]
            message[4, HEAD:, one(v)] = jnp.zeros((MSG - HEAD, LANES), jnp.float32)
            return carry

        lax.fori_loop(0, NV, close_one, 0)
        close.start()

    def chunk_of(c, carry):
        rows = pl.ds(pl.multiple_of(c * CHUNK, 16), CHUNK)

        @pl.when(c == 1)
        def _():
            loads[6].wait()

        def local_pair(k, carry):
            lanes = pair(k)
            local[rows, lanes] = jnp.dot(
                body_op[rows, :], box[:, lanes], preferred_element_type=jnp.float32
            )
            return carry

        lax.fori_loop(0, pairs, local_pair, 0)

        @pl.when(c < 2)
        def _():
            lax.fori_loop(2 * c, 2 * c + 2, send_face, 0)

        @pl.when(jnp.logical_and(c == 1, is_end))
        def _():
            close_end()

        return carry

    lax.fori_loop(0, TABLE // CHUNK, chunk_of, 0)

    def make_inner(k, carry):
        end, v = k // NV, lax.rem(k, NV)
        make_message(local, Z_FACE + end * BLOCK, 2, end, v, z_message, end)
        return carry

    lax.fori_loop(0, 2 * NV, make_inner, 0)
    lane = lax.broadcasted_iota(jnp.int32, (MSG, LANES), 1)

    def fill_z(v, carry):
        lanes = one(v)
        closing = half_gain * half_gain * viscosity[v]
        blank = jnp.zeros((MSG - HEAD, LANES), jnp.float32)
        sides = []
        for end, (edge_lane, by) in enumerate(((0, 1), (LANES - 1, LANES - 1))):
            at = Z_FACE + end * BLOCK
            outside = jnp.concatenate([closing * local[at : at + HEAD, lanes], blank], axis=0)
            inside = pltpu.roll(z_message[1 - end, :, lanes], by, 1)
            sides.append(jnp.where(lane == edge_lane, outside, inside))
        put_box(far_box, lanes, jnp.concatenate(sides, axis=0))
        return carry

    loads[8].wait()
    rows_at_once = 24

    def mix_rows(k, carry):
        rows = pl.ds(pl.multiple_of(k * rows_at_once, 8), rows_at_once)
        weight = -speed[0] * edge[0, rows]
        for d in range(1, 3):
            weight = weight - speed[d] * edge[d, rows]

        def mix(v, carry):
            lanes = one(v)
            at = pl.ds(pl.multiple_of(OWN + 3 * BODY + k * rows_at_once, 8), rows_at_once)
            mixed = weight * state[v, rows] + viscosity[v] * local[at, lanes]
            for d in range(3):
                at = pl.ds(pl.multiple_of(OWN + d * BODY + k * rows_at_once, 8), rows_at_once)
                for w in range(NV):
                    mixed = mixed - flux[d, v, w] * local[at, columns(w)]
            total[rows, lanes] = mixed
            return carry

        return lax.fori_loop(0, NV, mix, carry)

    lax.fori_loop(0, BODY // rows_at_once, mix_rows, 0)

    loads[7].wait()
    loads[9].wait()

    def take_along():
        @pl.when(is_mortar)
        def _():
            for send, up, down in pieces:
                send.wait_recv()
                up.start()
                down.start()

        go_after.wait()
        go_before.wait()

    def take_axis():
        @pl.when(has_right)
        def _():
            go_right.wait_send()
            remote(message.at[0], from_right, 1, me + 1, place).wait_recv()

        @pl.when(has_left)
        def _():
            go_left.wait_send()
            remote(message.at[1], from_left, 0, me - 1, place).wait_recv()

        @pl.when(is_end)
        def _():
            close.wait()

        @pl.when(is_mortar)
        def _():
            for send, up, down in pieces:
                send.wait_send()
                up.wait()
                down.wait()
            row_after.wait()
            row_before.wait()
            keep.wait()
            straight_low = jnp.where(is_rotor, odd[0], 1 - odd[0])

            def fill_mortar(v, carry):
                put_box(mortar_box, one(v), mortar_in[:, one(v)])
                return carry

            lax.fori_loop(0, NV, fill_mortar, 0)

            def stand_pair(k, carry):
                lanes = pair(k)
                stand_in[:, lanes] = jnp.dot(
                    mortar_op[straight_low], mortar_box[:, lanes], preferred_element_type=jnp.float32
                )
                return carry

            lax.fori_loop(0, pairs, stand_pair, 0)
            slot_rows = pl.ds(pl.multiple_of(own * MSG, 8), MSG)
            for v in range(NV):
                inbox[slot_rows, columns(v)] = stand_in[:MSG, columns(v)]

    def add_far(stage, carry):
        d = 2 - stage

        @pl.when(stage == 0)
        def _():
            lax.fori_loop(0, NV, fill_z, 0)

        @pl.when(stage == 1)
        def _():
            take_along()

        @pl.when(stage == 2)
        def _():
            take_axis()

        @pl.when(stage > 0)
        def _():
            first_row = pl.multiple_of(d * 2 * MSG, 8)

            def fill(v, carry):
                put_box(far_box, one(v), inbox[pl.ds(first_row, 2 * MSG), one(v)])
                return carry

            lax.fori_loop(0, NV, fill, 0)

        def add(k, carry):
            lanes = pair(k)
            term = jnp.dot(far_op[d], far_box[:, lanes], preferred_element_type=jnp.float32)
            total[:, lanes] += term[:BODY]
            return carry

        return lax.fori_loop(0, pairs, add, carry)

    lax.fori_loop(0, 3, add_far, 0)
    store = pltpu.make_async_copy(total.at[:, 0:WIDE], residual_hbm, local_sem.at[2])
    store.start()
    store.wait()


def finish(state, register, residual, state_new, register_new):
    for v in range(NV):
        fresh = section_a * register[v] + residual[:, columns(v)]
        register_new[v] = fresh
        state_new[v] = state[v] + (section_b * step_size) * fresh


def on_device(counts, tables, state, register, flux_x, flux_y, flux_z, viscosity, mortar_partner):
    axial_count, sectors = counts
    body, far, mortar, edge = tables
    flat = state.reshape((NV, BODY, LANES))
    flat_register = register.reshape((NV, BODY, LANES))
    vmem = pl.BlockSpec(memory_space=pltpu.VMEM)
    hbm = pl.BlockSpec(memory_space=pltpu.HBM)
    smem = pl.BlockSpec(memory_space=pltpu.SMEM)
    limit = 48 * 1024 * 1024

    shift = lax.rem(mortar_partner[0, 0] - lax.axis_index("sector") + sectors, sectors)

    def run(which):
        return pl.pallas_call(
            functools.partial(exchange, which, counts),
            out_shape=jax.ShapeDtypeStruct((BODY, WIDE), jnp.float32),
            in_specs=[smem] + [hbm] * 9,
            out_specs=hbm,
            scratch_shapes=[
                pltpu.VMEM((NV, BODY, LANES), jnp.float32),
                pltpu.VMEM(body.shape, jnp.bfloat16),
                pltpu.VMEM(far.shape, jnp.bfloat16),
                pltpu.VMEM(mortar.shape, jnp.bfloat16),
                pltpu.VMEM(edge.shape, jnp.float32),
                pltpu.SMEM((3, NV, NV), jnp.float32),
                pltpu.SMEM((NV,), jnp.float32),
                pltpu.SMEM((3,), jnp.float32),
                pltpu.VMEM((5, MSG, WIDE), jnp.float32),
                pltpu.VMEM((3 * BODY_PAD, ROOM), jnp.bfloat16),
                pltpu.VMEM((4 * MSG, WIDE), jnp.float32),
                pltpu.VMEM((MORT_K, WIDE), jnp.float32),
                pltpu.VMEM((3 * MORT_K, ROOM), jnp.bfloat16),
                pltpu.VMEM((80, ROOM), jnp.float32),
                pltpu.VMEM((2, MSG, WIDE), jnp.float32),
                pltpu.VMEM((6 * MSG, ROOM), jnp.bfloat16),
                pltpu.VMEM((TABLE, ROOM), jnp.float32),
                pltpu.VMEM((BODY, ROOM), jnp.float32),
                pltpu.SemaphoreType.DMA((10,)),
                pltpu.SemaphoreType.DMA((3,)),
                pltpu.SemaphoreType.DMA((12,)),
                pltpu.SemaphoreType.DMA((12,)),
            ],
            compiler_params=pltpu.CompilerParams(
                collective_id=which, has_side_effects=True, vmem_limit_bytes=limit
            ),
            name=f"exchange_{which}",
        )

    residual = lax.switch(
        shift // 2,
        [run(which) for which in range(sectors // 2)],
        lax.rem(shift, 2).reshape((1,)),
        flat,
        body,
        far,
        mortar,
        edge,
        flux_x,
        flux_y,
        flux_z,
        viscosity,
    )

    whole = jax.ShapeDtypeStruct((NV, BODY, LANES), jnp.float32)
    state_new, register_new = pl.pallas_call(
        finish,
        out_shape=(whole, whole),
        in_specs=[vmem] * 3,
        out_specs=(vmem, vmem),
        name="finish",
    )(flat, flat_register, residual)
    return (state_new.reshape(state.shape), register_new.reshape(state.shape))


def solution(mesh):
    counts = (mesh.shape["axial"], mesh.shape["sector"])
    face, body, far, mortar = operators()
    edge = np.zeros((3, BODY, LANES), np.float32)
    ends = np.zeros(NN)
    ends[0] = ends[-1] = 1.0
    for d in range(3):
        edge[d] = np.diag(along(np.diag(ends), d))[:, None]
    tables = tuple(
        jnp.asarray(table)
        for table in (
            thirds(np.concatenate([face, body])),
            thirds(far),
            thirds(mortar),
            edge,
        )
    )
    spec = P(None, None, None, None, "axial", "sector", None)
    return jax.shard_map(
        functools.partial(on_device, counts, tables),
        mesh=mesh,
        in_specs=(spec, spec, P(), P(), P(), P(), P(None, "sector")),
        out_specs=(spec, spec),
        check_vma=False,
    )
```

profile of v0, /device:TPU:32, one launch (start us, length us, event | category | flops | bytes accessed | tf_op | source)
XLA Modules:
  0.0 34.4 jit_solution(3768988614737569827)
XLA Ops:
  1.3 30.7 %conditional.1 = (f32[216,640]{1,0:T(8,128)S(1)}) conditional(s32[]{:T(128)} %clamp.3, (s32[1]{0:T(128)}, f32[5,216,128]{2,1,0:T(8,128)}, bf16[1536,672]{1,0:T(8,128)(2,1)}, bf16[3,224,432]{2,1,0:T(8,128)(2,1)}, bf16[2,80,1104]{2,1,0:T(8,128)(2,1)}, /*index=5*/f32[3,216,128]{2,1,0:T(8,128)}, f32[5,5]{1,0:T(8,128)}, ...), branch_computations={%region_0.1_spmd, %region_1.2_spmd, %region_2.3_spmd, %region_3.4_... | conditional | bytes 8 | solution.py:633
  1.4 30.3 %exchange_9.1 = f32[216,640]{1,0:T(8,128)S(1)} custom-call(s32[1]{0:T(128)} %get-tuple-element.427.odd, f32[5,216,128]{2,1,0:T(8,128)} %get-tuple-element.428.state_hbm, bf16[1536,672]{1,0:T(8,128)(2,1)} %get-tuple-element.429.body_hbm, bf16[3,224,432]{2,1,0:T(8,128)(2,1)} %get-tuple-element.430.far_hbm, bf16[2,80,1104]{2,1,0:T(8,128)(2,1)} %get-tuple-element.431.mortar_hbm, ...), custom_call_target="tpu_custom_call" | custom-call | tf_op jit(solution)/shard_map/cond/branch_9_fun/exchange_9/pallas_call | solution.py:633
  32.0 2.3 %finish.1 = (f32[5,216,128]{2,1,0:T(8,128)}, f32[5,216,128]{2,1,0:T(8,128)}) custom-call(f32[5,216,128]{2,1,0:T(8,128)} %bitcast.23, f32[5,216,128]{2,1,0:T(8,128)} %bitcast.24, f32[216,640]{1,0:T(8,128)S(1)} %get-tuple-element.507.residual), custom_call_target="tpu_custom_call" | custom-call | tf_op jit(solution)/shard_map/finish/pallas_call | solution.py:649
where the time goes:
time: 34.5 us; the launch traced here: 34.4 us
  Pallas kernels  32.6 us (94%)
  between operations  1.32 us (4%)
  loops' own time  0.46 us (1%)
    pallas_call x1, Pallas kernels, on_device(): lax.switch(shift // 2, [run(which) for which in range(sectors // 2)], lax...  30.3 us
    pallas_call x1, Pallas kernels, on_device(): pl.pallas_call(finish, out_shape=(whole, whole), in_specs=[vmem] * 3, out...  2.32 us

commit v1 on v0

--- a/solution.py
+++ b/solution.py
@@ -412,14 +412,9 @@
         def _():
             loads[6].wait()
 
-        def local_pair(k, carry):
-            lanes = pair(k)
-            local[rows, lanes] = jnp.dot(
-                body_op[rows, :], box[:, lanes], preferred_element_type=jnp.float32
-            )
-            return carry
-
-        lax.fori_loop(0, pairs, local_pair, 0)
+        local[rows, 0:WIDE] = jnp.dot(
+            body_op[rows, :], box[:, 0:WIDE], preferred_element_type=jnp.float32
+        )
 
         @pl.when(c < 2)
         def _():
@@ -561,13 +556,9 @@
 
             lax.fori_loop(0, NV, fill, 0)
 
-        def add(k, carry):
-            lanes = pair(k)
-            term = jnp.dot(far_op[d], far_box[:, lanes], preferred_element_type=jnp.float32)
-            total[:, lanes] += term[:BODY]
-            return carry
-
-        return lax.fori_loop(0, pairs, add, carry)
+        term = jnp.dot(far_op[d], far_box[:, 0:WIDE], preferred_element_type=jnp.float32)
+        total[:, 0:WIDE] += term[:BODY]
+        return carry
 
     lax.fori_loop(0, 3, add_far, 0)
     store = pltpu.make_async_copy(total.at[:, 0:WIDE], residual_hbm, local_sem.at[2])

time: 34.5 us -> 30.9 us (0.90); the launches traced: 34.4 us -> 31.3 us
  Pallas kernels: 32.6 us -> 29.7 us
    pallas_call x1, Pallas kernels: 30.3 us -> 27.4 us  [on_device(): lax.switch(shift // 2, [run(which) for which in range(sectors // 2)], lax...]
where the time goes in v1:
time: 30.9 us; the launch traced here: 31.3 us
  Pallas kernels  29.7 us (96%)
  between operations  1.32 us (4%)
    pallas_call x1, Pallas kernels, on_device(): lax.switch(shift // 2, [run(which) for which in range(sectors // 2)], lax...  27.4 us
    pallas_call x1, Pallas kernels, on_device(): pl.pallas_call(finish, out_shape=(whole, whole), in_specs=[vmem] * 3, out...  2.32 us

profile of v1, /device:TPU:32, one launch (start us, length us, event | category | flops | bytes accessed | tf_op | source)
XLA Modules:
  0.0 31.3 jit_solution(16276766489267570581)
XLA Ops:
  1.3 27.7 %conditional.1 = (f32[216,640]{1,0:T(8,128)S(1)}) conditional(s32[]{:T(128)} %clamp.3, (s32[1]{0:T(128)}, f32[5,216,128]{2,1,0:T(8,128)}, bf16[1536,672]{1,0:T(8,128)(2,1)}, bf16[3,224,432]{2,1,0:T(8,128)(2,1)}, bf16[2,80,1104]{2,1,0:T(8,128)(2,1)}, /*index=5*/f32[3,216,128]{2,1,0:T(8,128)}, f32[5,5]{1,0:T(8,128)}, ...), branch_computations={%region_0.1_spmd, %region_1.2_spmd, %region_2.3_spmd, %region_3.4_... | conditional | bytes 8 | solution.py:624
  1.5 27.4 %exchange_8.1 = f32[216,640]{1,0:T(8,128)S(1)} custom-call(s32[1]{0:T(128)} %get-tuple-element.417.odd, f32[5,216,128]{2,1,0:T(8,128)} %get-tuple-element.418.state_hbm, bf16[1536,672]{1,0:T(8,128)(2,1)} %get-tuple-element.419.body_hbm, bf16[3,224,432]{2,1,0:T(8,128)(2,1)} %get-tuple-element.420.far_hbm, bf16[2,80,1104]{2,1,0:T(8,128)(2,1)} %get-tuple-element.421.mortar_hbm, ...), custom_call_target="tpu_custom_call" | custom-call | tf_op jit(solution)/shard_map/cond/branch_8_fun/exchange_8/pallas_call | solution.py:624
  29.0 2.3 %finish.1 = (f32[5,216,128]{2,1,0:T(8,128)}, f32[5,216,128]{2,1,0:T(8,128)}) custom-call(f32[5,216,128]{2,1,0:T(8,128)} %bitcast.23, f32[5,216,128]{2,1,0:T(8,128)} %bitcast.24, f32[216,640]{1,0:T(8,128)S(1)} %get-tuple-element.507.residual), custom_call_target="tpu_custom_call" | custom-call | tf_op jit(solution)/shard_map/finish/pallas_call | solution.py:640
